TPU v7x, 256 devices: a whole 4x4x8 slice. The times are simulated.
256 devices in a mesh: blk: 32 (over z, y_lo, core), dp: 8 (over x, y_hi).
Axes of the slice: x: 4, y: 4 (y_hi: 2, y_lo: 2; y = y_hi * 2 + y_lo), z: 8, core: 2. Of those that a mesh axis runs over, the one named last changes fastest.
Arguments:
- images: bfloat16 [131072, 1152], P(('blk', 'dp')), may hold values from -4 to 4
- texts: bfloat16 [131072, 1152], P(('blk', 'dp')), may hold values from -4 to 4
- positives: int32 [256, 512], P(('blk', 'dp')), may hold values from 0 to 511, as said below
- log_scale: float32 [1], replicated, may hold values from 2.08 to 2.48
- bias: float32 [1], replicated, may hold values from -9 to -7
Outputs:
- image_grad: bfloat16 [131072, 1152], P(('blk', 'dp'))
- text_grad: bfloat16 [131072, 1152], P(('blk', 'dp'))
- totals: float32 [3], replicated
Inputs may be any that keep to these rules, and one draw needn't show every extreme that they name: `positives`: each row orders 0 to 511, each once.
All inputs are finite; a program needn't handle non-finite values.
Results may differ from a plain program's by a relative error of at most 0.0056.
Values may be sent and summed in bfloat16 or wider, within the bound.
A program may use at most 64 MiB of HBM per device.

v0:
```python
import jax
import jax.numpy as jnp
from jax import lax
from jax.sharding import PartitionSpec as P

STEPS = 4


def from_behind(value, axis, by):
    devices = lax.axis_size(axis)
    return lax.ppermute(value, axis, [(i, (i + by) % devices) for i in range(devices)])


def normalize(raw):
    full = raw.astype(jnp.float32)
    factor = lax.rsqrt(jnp.sum(full * full, axis=-1, keepdims=True) + 1e-06)
    return (full * factor, factor)


def backnorm(grad, unit, factor):
    return factor * (grad - unit * jnp.sum(unit * grad, axis=-1, keepdims=True))


def tile_terms(rows_half, cols_half, sign, scale, shift):
    logits = (
        scale
        * lax.dot_general(
            rows_half, cols_half, (((1,), (1,)), ((), ())), preferred_element_type=jnp.float32
        )
        + shift
    )
    coeff = -sign * jax.nn.sigmoid(-sign * logits)
    return (logits, coeff)


def column_product(coeff_half, rows_half):
    return lax.dot_general(
        coeff_half, rows_half, (((0,), (0,)), ((), ())), preferred_element_type=jnp.float32
    )


def body(images, texts, positives, log_scale, bias):
    scale = jnp.exp(log_scale[0])
    shift = bias[0]
    x_full, x_factor = normalize(images)
    y_full, y_factor = normalize(texts)
    x_half = x_full.astype(jnp.bfloat16)
    y_half = y_full.astype(jnp.bfloat16)
    width = images.shape[0]
    columns = lax.broadcasted_iota(jnp.int32, (width, width), 1)
    first_sign = jnp.where(positives[0][:, None] == columns, 1.0, -1.0).astype(jnp.float32)
    held = y_half
    image_sum = jnp.zeros(images.shape, jnp.float32)
    text_sum = jnp.zeros(texts.shape, jnp.float32)
    loss_sum = jnp.float32(0.0)
    coeff_sum = jnp.float32(0.0)
    logit_sum = jnp.float32(0.0)
    for step in range(STEPS):
        sign = first_sign if step == 0 else jnp.float32(-1.0)
        if step > 0:
            held = from_behind(held, "blk", 1)
        logits, coeff = tile_terms(x_half, held, sign, scale, shift)
        loss_sum = loss_sum + jnp.sum(jax.nn.softplus(-sign * logits))
        coeff_sum = coeff_sum + jnp.sum(coeff)
        logit_sum = logit_sum + jnp.sum(coeff * (logits - shift))
        coeff_half = coeff.astype(jnp.bfloat16)
        image_sum = image_sum + jnp.dot(coeff_half, held, preferred_element_type=jnp.float32)
        if step > 0:
            text_sum = from_behind(text_sum, "blk", 1)
        text_sum = text_sum + column_product(coeff_half, x_half)
    text_sum = from_behind(text_sum, "blk", -(STEPS - 1))
    summed = lax.psum((loss_sum, logit_sum, coeff_sum), ("blk", "dp"))
    count = jnp.float32(width * lax.axis_size("blk") * lax.axis_size("dp"))
    totals = jnp.stack([summed[0], summed[1], summed[2]]) / count
    image_grad = backnorm(scale * image_sum, x_full, x_factor)
    text_grad = backnorm(scale * text_sum, y_full, y_factor)
    return (image_grad.astype(jnp.bfloat16), text_grad.astype(jnp.bfloat16), totals)


def solution(mesh):
    return jax.shard_map(
        body,
        mesh=mesh,
        in_specs=(P(("blk", "dp"), None), P(("blk", "dp"), None), P(("blk", "dp"), None), P(), P()),
        out_specs=(P(("blk", "dp"), None), P(("blk", "dp"), None), P()),
        check_vma=False,
    )
```

profile of v0, /device:TPU:9, one launch (start us, length us, event | category | flops | bytes accessed | tf_op | source)
XLA Modules:
  0.0 259.8 jit_solution(759776880419109343)
XLA Ops:
  0.6 0.0 copy-start.1
  0.6 0.0 copy-start
  0.7 0.0 copy-start.6
  0.7 1.7 fusion.11
  2.4 1.6 fusion.16
  4.0 0.0 copy-done
  4.0 0.3 fusion.3
  5.6 0.0 copy-done.1
  5.6 0.0 copy-done.6
  5.6 2.6 %fusion.21 = (f32[]{:T(128)}, f32[]{:T(128)}, f32[]{:T(128)}, f32[512,512]{1,0:T(8,128)S(1)}) fusion(s32[512]{0:T(512)S(1)} %bitcast.18, f32[]{:T(128)} %bitcast.14, bf16[512,1152]{1,0:T(8,128)(2,1)S(1)} %fusion.3, bf16[512,1152]{1,0:T(8,128)(2,1)S(1)} %copy-done.1, f32[512]{0:T(512)S(1)} %add_rsqrt_fusion.1, f32[]{:T(128)} %bitcast), kind=kOutput, calls=%fused_computation.37 | convolution fusion | flops 611254272 | bytes 3411988 | tf_op jit(solution)/shard_map/dot_general | solution.py:27
  8.3 1.2 fusion.34
  9.4 2.2 collective-permute-start.3
  11.6 0.1 collective-permute-start
  11.7 38.3 %collective-permute-done = bf16[512,1152]{1,0:T(8,128)(2,1)S(1)} collective-permute-done((bf16[512,1152]{1,0:T(8,128)(2,1)S(1)}, bf16[512,1152]{1,0:T(8,128)(2,1)S(1)}, u32[]{:S(2)}, u32[]{:S(2)}) %collective-permute-start) | collective-permute-done | bytes 1179680 | tf_op jit(solution)/shard_map/ppermute | solution.py:11
  50.0 0.0 copy-start.3
  50.0 2.4 fusion.22
  52.5 0.0 copy-start.7
  52.5 0.0 collective-permute-done.3
  52.5 1.0 convolution_add_fusion
  53.5 0.0 copy-done.7
  53.5 3.4 %collective-permute-start.4 = (f32[512,1152]{1,0:T(8,128)S(1)}, f32[512,1152]{1,0:T(8,128)S(1)}, u32[]{:S(2)}, u32[]{:S(2)}) collective-permute-start(f32[512,1152]{1,0:T(8,128)S(1)} %convolution_add_fusion), channel_id=1, source_target_pairs={{0,8},{8,16},{16,24},{24,32},{32,40},{40,48},{48,56},{56,64},{64,7... | collective-permute-start | bytes 7077896 | tf_op jit(solution)/shard_map/ppermute | solution.py:11
  57.0 0.0 copy-done.3
  57.0 0.3 collective-permute-start.1
  57.2 38.1 %collective-permute-done.1 = bf16[512,1152]{1,0:T(8,128)(2,1)S(1)} collective-permute-done((bf16[512,1152]{1,0:T(8,128)(2,1)S(1)}, bf16[512,1152]{1,0:T(8,128)(2,1)S(1)}, u32[]{:S(2)}, u32[]{:S(2)}) %collective-permute-start.1) | collective-permute-done | bytes 1179680 | tf_op jit(solution)/shard_map/ppermute | solution.py:11
  95.4 0.0 copy-start.5
  95.4 2.4 fusion.23
  97.8 0.0 copy-start.8
  97.8 1.0 fusion.29
  98.8 0.0 copy-done.8
  98.8 0.0 collective-permute-done.4
  98.8 0.2 add.125
  99.1 3.5 %collective-permute-start.5 = (f32[512,1152]{1,0:T(8,128)S(1)}, f32[512,1152]{1,0:T(8,128)S(1)}, u32[]{:S(2)}, u32[]{:S(2)}) collective-permute-start(f32[512,1152]{1,0:T(8,128)S(1)} %add.125), channel_id=1, source_target_pairs={{0,8},{8,16},{16,24},{24,32},{32,40},{40,48},{48,56},{56,64},{64,7... | collective-permute-start | bytes 7077896 | tf_op jit(solution)/shard_map/ppermute | solution.py:11
  102.5 0.0 copy-done.5
  102.5 0.1 collective-permute-start.2
  102.6 38.3 %collective-permute-done.2 = bf16[512,1152]{1,0:T(8,128)(2,1)S(1)} collective-permute-done((bf16[512,1152]{1,0:T(8,128)(2,1)S(1)}, bf16[512,1152]{1,0:T(8,128)(2,1)S(1)}, u32[]{:S(2)}, u32[]{:S(2)}) %collective-permute-start.2) | collective-permute-done | bytes 1179680 | tf_op jit(solution)/shard_map/ppermute | solution.py:11
  141.0 0.0 copy-start.4
  141.0 2.4 fusion.24
  143.4 0.0 copy-done.4
  143.4 0.0 copy-start.9
  143.4 1.0 fusion.26
  144.4 0.0 copy-done.9
  144.4 0.0 collective-permute-done.5
  144.4 1.7 add.126
  146.1 8.1 %collective-permute-start.6 = (f32[512,1152]{1,0:T(8,128)}, f32[512,1152]{1,0:T(8,128)S(1)}, u32[]{:S(2)}, u32[]{:S(2)}) collective-permute-start(f32[512,1152]{1,0:T(8,128)} %add.126), channel_id=1, source_target_pairs={{0,232},{8,240},{16,248},{24,0},{32,8},{40,16},{48,24},{56,32},{64... | collective-permute-start | bytes 7077896 | tf_op jit(solution)/shard_map/ppermute | solution.py:11
  154.2 2.5 fusion.36
  160.4 4.6 %convolution_add_fusion.3 = f32[512,1152]{1,0:T(8,128)} fusion(f32[512,1152]{1,0:T(8,128)} %fusion.36, bf16[512,1152]{1,0:T(8,128)(2,1)} %copy-done.3, f32[512,512]{1,0:T(8,128)} %copy-done.7), kind=kOutput, calls=%fused_computation.3 | convolution fusion | flops 605618176 | bytes 6946816 | tf_op jit(solution)/shard_map/dot_general | solution.py:67
  166.8 4.6 %convolution_add_fusion.2 = f32[512,1152]{1,0:T(8,128)} fusion(f32[512,1152]{1,0:T(8,128)} %convolution_add_fusion.3, bf16[512,1152]{1,0:T(8,128)(2,1)} %copy-done.5, f32[512,512]{1,0:T(8,128)} %copy-done.8), kind=kOutput, calls=%fused_computation.2 | convolution fusion | flops 605618176 | bytes 6946816 | tf_op jit(solution)/shard_map/dot_general | solution.py:67
  173.2 76.7 %all-reduce = (f32[1]{0:T(128)}, f32[1]{0:T(128)}, f32[1]{0:T(128)}) all-reduce(f32[1]{0:T(128)} %bitcast.5, f32[1]{0:T(128)} %bitcast.4, f32[1]{0:T(128)} %bitcast.3), channel_id=1, replica_groups=mesh['blk'=32,'dp'=8] {'blk','dp'}, use_global_device_ids=true, to_apply=%region_18.19 | all-reduce | flops 3 | bytes 24 | tf_op jit(solution)/shard_map/psum | solution.py:72
  249.9 2.5 maximum_multiply_fusion
  252.4 0.0 copy-start.2
  252.4 3.8 %fusion.7 = (f32[512]{0:T(512)S(1)}, f32[512,1152]{1,0:T(8,128)S(1)}) fusion(bf16[512,1152]{1,0:T(8,128)(2,1)} %param.5, f32[512]{0:T(512)S(1)} %add_rsqrt_fusion.1, f32[512,1152]{1,0:T(8,128)} %convolution_add_fusion.2, bf16[512,1152]{1,0:T(8,128)(2,1)} %copy-done.4, f32[512,512]{1,0:T(8,128)} %copy-done.9, f32[]{:T(128)} %bitcast), kind=kOutput, calls=%fused_computation.19 | convolution fusion | flops 608566784 | bytes 8130564 | tf_op jit(solution)/shard_map/dot_general | solution.py:67
  256.1 0.0 copy-done.2
  256.1 1.5 fusion.10
  257.7 0.0 collective-permute-done.6
  257.7 0.5 fusion.12
  258.2 1.6 fusion.15
  (2 shorter events, 0.0 us)
Async XLA Ops:
  0.6 5.0 %copy-start.1 = (bf16[512,1152]{1,0:T(8,128)(2,1)S(1)}, bf16[512,1152]{1,0:T(8,128)(2,1)}, u32[]{:S(2)}) copy-start(bf16[512,1152]{1,0:T(8,128)(2,1)} %param.5) | copy-start | bytes 3538948
  0.6 3.3 %copy-start = (bf16[512,1152]{1,0:T(8,128)(2,1)S(1)}, bf16[512,1152]{1,0:T(8,128)(2,1)}, u32[]{:S(2)}) copy-start(bf16[512,1152]{1,0:T(8,128)(2,1)} %param.6) | copy-start | bytes 3538948
  0.7 5.0 %copy-start.6 = (s32[1,512]{1,0:T(1,128)S(1)}, s32[1,512]{1,0:T(1,128)}, u32[]{:S(2)}) copy-start(s32[1,512]{1,0:T(1,128)} %param.7) | copy-start | bytes 6148
  9.4 43.0 %collective-permute-start.3 = (f32[512,1152]{1,0:T(8,128)S(1)}, f32[512,1152]{1,0:T(8,128)S(1)}, u32[]{:S(2)}, u32[]{:S(2)}) collective-permute-start(f32[512,1152]{1,0:T(8,128)S(1)} %fusion.34), channel_id=1, source_target_pairs={{0,8},{8,16},{16,24},{24,32},{32,40},{40,48},{48,56},{56,64},{64,7... | collective-permute-start | bytes 7077896 | tf_op jit(solution)/shard_map/ppermute | solution.py:11
  11.6 38.4 %collective-permute-start = (bf16[512,1152]{1,0:T(8,128)(2,1)S(1)}, bf16[512,1152]{1,0:T(8,128)(2,1)S(1)}, u32[]{:S(2)}, u32[]{:S(2)}) collective-permute-start(bf16[512,1152]{1,0:T(8,128)(2,1)S(1)} %fusion.3), channel_id=1, source_target_pairs={{0,8},{8,16},{16,24},{24,32},{32,40},{40,48},{48,56},{56,64},{64,7... | collective-permute-start | bytes 3538952 | tf_op jit(solution)/shard_map/ppermute | solution.py:11
  50.0 6.9 %copy-start.3 = (bf16[512,1152]{1,0:T(8,128)(2,1)}, bf16[512,1152]{1,0:T(8,128)(2,1)S(1)}, u32[]{:S(2)}) copy-start(bf16[512,1152]{1,0:T(8,128)(2,1)S(1)} %collective-permute-done) | copy-start | bytes 3538948
  52.5 1.1 copy-start.7
  53.5 45.3 %collective-permute-start.4 = (f32[512,1152]{1,0:T(8,128)S(1)}, f32[512,1152]{1,0:T(8,128)S(1)}, u32[]{:S(2)}, u32[]{:S(2)}) collective-permute-start(f32[512,1152]{1,0:T(8,128)S(1)} %convolution_add_fusion), channel_id=1, source_target_pairs={{0,8},{8,16},{16,24},{24,32},{32,40},{40,48},{48,56},{56,64},{64,7... | collective-permute-start | bytes 7077896 | tf_op jit(solution)/shard_map/ppermute | solution.py:11
  57.0 38.4 %collective-permute-start.1 = (bf16[512,1152]{1,0:T(8,128)(2,1)S(1)}, bf16[512,1152]{1,0:T(8,128)(2,1)S(1)}, u32[]{:S(2)}, u32[]{:S(2)}) collective-permute-start(bf16[512,1152]{1,0:T(8,128)(2,1)S(1)} %collective-permute-done), channel_id=1, source_target_pairs={{0,8},{8,16},{16,24},{24,32},{32,40},{40,48},{48,56},{56,64},{64,7... | collective-permute-start | bytes 3538952 | tf_op jit(solution)/shard_map/ppermute | solution.py:11
  95.4 7.1 %copy-start.5 = (bf16[512,1152]{1,0:T(8,128)(2,1)}, bf16[512,1152]{1,0:T(8,128)(2,1)S(1)}, u32[]{:S(2)}) copy-start(bf16[512,1152]{1,0:T(8,128)(2,1)S(1)} %collective-permute-done.1) | copy-start | bytes 3538948
  97.8 1.0 copy-start.8
  99.1 45.4 %collective-permute-start.5 = (f32[512,1152]{1,0:T(8,128)S(1)}, f32[512,1152]{1,0:T(8,128)S(1)}, u32[]{:S(2)}, u32[]{:S(2)}) collective-permute-start(f32[512,1152]{1,0:T(8,128)S(1)} %add.125), channel_id=1, source_target_pairs={{0,8},{8,16},{16,24},{24,32},{32,40},{40,48},{48,56},{56,64},{64,7... | collective-permute-start | bytes 7077896 | tf_op jit(solution)/shard_map/ppermute | solution.py:11
  102.5 38.4 %collective-permute-start.2 = (bf16[512,1152]{1,0:T(8,128)(2,1)S(1)}, bf16[512,1152]{1,0:T(8,128)(2,1)S(1)}, u32[]{:S(2)}, u32[]{:S(2)}) collective-permute-start(bf16[512,1152]{1,0:T(8,128)(2,1)S(1)} %collective-permute-done.1), channel_id=1, source_target_pairs={{0,8},{8,16},{16,24},{24,32},{32,40},{40,48},{48,56},{56,64},{64,7... | collective-permute-start | bytes 3538952 | tf_op jit(solution)/shard_map/ppermute | solution.py:11
  141.0 2.4 copy-start.4
  143.4 1.0 copy-start.9
  146.1 111.6 %collective-permute-start.6 = (f32[512,1152]{1,0:T(8,128)}, f32[512,1152]{1,0:T(8,128)S(1)}, u32[]{:S(2)}, u32[]{:S(2)}) collective-permute-start(f32[512,1152]{1,0:T(8,128)} %add.126), channel_id=1, source_target_pairs={{0,232},{8,240},{16,248},{24,0},{32,8},{40,16},{48,24},{56,32},{64... | collective-permute-start | bytes 7077896 | tf_op jit(solution)/shard_map/ppermute | solution.py:11
  252.4 3.8 %copy-start.2 = (bf16[512,1152]{1,0:T(8,128)(2,1)S(1)}, bf16[512,1152]{1,0:T(8,128)(2,1)}, u32[]{:S(2)}) copy-start(bf16[512,1152]{1,0:T(8,128)(2,1)} %param.5) | copy-start | bytes 3538948
where the time goes:
time: 263 us; the launch traced here: 260 us
  waiting for transfers between devices  115 us (44%)
  blocking collectives  76.7 us (29%)
  matrix products  29.6 us (11%)
  starting transfers between devices  17.6 us (7%)
  other arithmetic  11.7 us (4%)
  between operations  9.32 us (4%)
    ppermute x7, waiting for transfers between devices, from_behind(): lax.ppermute(value, axis, [(i, (i + by) % devices) for i in range(devices)])  115 us
    psum x1, blocking collectives, body(): summed = lax.psum((loss_sum, logit_sum, coeff_sum), ('blk', 'dp'))  76.7 us
    ppermute x7, starting transfers between devices, from_behind(): lax.ppermute(value, axis, [(i, (i + by) % devices) for i in range(devices)])  17.6 us
    dot_general x4, matrix products, body(): jnp.dot(coeff_half, held, preferred_element_type=jnp.float32)  15.5 us
    dot_general x4, matrix products, tile_terms(): lax.dot_general(rows_half, cols_half, (((1,), (1,)), ((), ())), preferred...  9.86 us
  transfers between devices with their start and end apart: 7, of which 3 were waited for; matrix products, arithmetic and copies ran while one was open for 11% of the time, Pallas kernels for 0%

commit v1 on v0

v1 whole, which is shorter than its diff:
```python
import jax
import jax.numpy as jnp
from jax import lax
from jax.experimental import pallas as pl
from jax.experimental.pallas import tpu as pltpu
from jax.sharding import PartitionSpec as P

MESH = pl.DeviceIdType.MESH
BF16 = jnp.bfloat16
F32 = jnp.float32

ROWS = 512
WIDTH = 1152
COUNT = 131072.0
N_BLK = 32
PIECE = 64
PIECES = ROWS // PIECE
STEPS = 2 * PIECES
TILE = 128
HALF = 256
WINDOW = 3
PARTNER = STEPS * 2 * PIECE
SKIP = PARTNER + ROWS


def contract_last(a, b):
    return lax.dot_general(a, b, (((1,), (1,)), ((), ())), preferred_element_type=F32)


def contract_first(a, b):
    return lax.dot_general(a, b, (((0,), (0,)), ((), ())), preferred_element_type=F32)


def fold(v):
    return jnp.sum(v.reshape(v.shape[0] // 8, 8, v.shape[1]), axis=0)


def kernel(
    images, texts, positives, log_scale, bias,
    image_grad, text_grad, totals,
    raw, unit, factor, total, held, result, sums, share,
    load_sem, link_send, link_recv, pass_send, pass_recv, pair_send, pair_recv,
    skip_send, skip_recv, share_send, share_recv, out_sem,
):
    k = lax.axis_index("blk")
    p = lax.axis_index("dp")
    core = lax.rem(k, 2)
    pair = k + 1 - 2 * core
    skip = lax.rem(k - 3 + 6 * core + N_BLK, N_BLK)

    def load(side):
        return pltpu.make_async_copy((images, texts)[side], raw.at[side], load_sem.at[side])

    load(1).start()
    load(0).start()

    def group(level, i):
        if level == 0:
            digit = lax.rem(k, 4)
            return (k - digit + lax.rem(digit + i, 4), p)
        if level == 1:
            digit = lax.rem(k // 4, 4)
            return (k + 4 * (lax.rem(digit + i, 4) - digit), p)
        if level == 2:
            digit = lax.rem(p, 4)
            return (k, p - digit + lax.rem(digit + i, 4))
        digit = 2 * (k // 16) + p // 4
        other = lax.rem(digit + i, 4)
        return (lax.rem(k, 16) + 16 * (other // 2), lax.rem(p, 4) + 4 * lax.rem(other, 2))

    barrier = pltpu.get_barrier_semaphore()
    greeted = [(lax.rem(k + 2, N_BLK), p), (lax.rem(k - 2 + N_BLK, N_BLK), p), (pair, p), (skip, p)]
    greeted += [group(level, i) for level in range(4) for i in (1, 2, 3)]
    for device in greeted:
        pl.semaphore_signal(barrier, inc=1, device_id=device, device_id_type=MESH)

    def link(t):
        second = t // PIECES
        start = pl.multiple_of(PIECE * lax.rem(t, PIECES), PIECE)
        place = pl.multiple_of(2 * PIECE * t, PIECE)
        return pltpu.make_async_remote_copy(
            src_ref=unit.at[1 - second, pl.ds(start, PIECE)],
            dst_ref=held.at[pl.ds(place, PIECE)],
            send_sem=link_send.at[t],
            recv_sem=link_recv.at[t],
            device_id=(lax.rem(k + 2 - 4 * second + N_BLK, N_BLK), p),
            device_id_type=MESH,
        )

    def hand_on(t):
        place = pl.multiple_of(2 * PIECE * t, PIECE)
        return pltpu.make_async_remote_copy(
            src_ref=held.at[pl.ds(place, PIECE)],
            dst_ref=held.at[pl.ds(place + PIECE, PIECE)],
            send_sem=pass_send.at[t],
            recv_sem=pass_recv.at[t],
            device_id=(pair, p),
            device_id_type=MESH,
        )

    to_pair = pltpu.make_async_remote_copy(
        src_ref=unit.at[1 - core],
        dst_ref=held.at[pl.ds(PARTNER, ROWS)],
        send_sem=pair_send,
        recv_sem=pair_recv,
        device_id=(pair, p),
        device_id_type=MESH,
    )

    def to_skip(q):
        start = pl.multiple_of(TILE * q, TILE)
        return pltpu.make_async_remote_copy(
            src_ref=unit.at[core, pl.ds(start, TILE)],
            dst_ref=held.at[pl.ds(SKIP + start, TILE)],
            send_sem=skip_send.at[q],
            recv_sem=skip_recv.at[q],
            device_id=(skip, p),
            device_id_type=MESH,
        )

    def normalize(side, j):
        rows = pl.ds(pl.multiple_of(PIECE * j, PIECE), PIECE)
        full = raw[side, rows, :].astype(F32)
        scaler = lax.rsqrt(jnp.sum(full * full, axis=-1, keepdims=True) + 1e-06)
        unit[side, rows, :] = (full * scaler).astype(BF16)
        factor[side, rows, :] = jnp.broadcast_to(scaler, (PIECE, 128))

    load(1).wait()
    normalize(1, 0)
    pl.semaphore_wait(barrier, len(greeted))
    link(0).start()
    for j in range(1, WINDOW):
        normalize(1, j)
        link(j).start()

    @pl.loop(WINDOW, PIECES)
    def _(j):
        normalize(1, j)

    pl.when(core == 0)(to_pair.start)
    load(0).wait()

    @pl.loop(0, PIECES)
    def _(j):
        normalize(0, j)

    pl.when(core == 1)(to_pair.start)

    @pl.when(core == 0)
    def _():
        for q in range(4):
            to_skip(q).start()

    scale = jnp.exp(jnp.full((1, 128), log_scale[0], F32))
    shift = bias[0]
    sums[...] = jnp.zeros_like(sums)

    def count(weight, loss, logit, coeff):
        sums[0] += weight * fold(loss)
        sums[1] += weight * fold(logit)
        sums[2] += weight * fold(coeff)

    @pl.loop(0, ROWS // TILE)
    def _(c):
        cols = pl.ds(pl.multiple_of(TILE * c, TILE), TILE)
        rows = unit[0, cols, :]
        wanted = positives[:, cols]
        halves = []
        for h in range(2):
            part = pl.ds(HALF * h, HALF)
            product = scale * contract_last(unit[1, part, :], rows)
            logits = product + shift
            match = lax.broadcasted_iota(jnp.int32, (HALF, TILE), 0) + HALF * h == wanted
            odds = jnp.exp(jnp.where(match, -logits, logits))
            chance = odds / (1.0 + odds)
            coeff = jnp.where(match, -chance, chance)
            count(1.0, jnp.log1p(odds), coeff * product, coeff)
            coeff = coeff.astype(BF16)
            halves.append(coeff)
            term = jnp.dot(coeff, rows, preferred_element_type=F32)

            @pl.when(c == 0)
            def _():
                total[1, part, :] = term

            @pl.when(c > 0)
            def _():
                total[1, part, :] += term

        total[0, cols, :] = contract_first(jnp.concatenate(halves, axis=0), unit[1])

    def work(side, place, weight):
        other = held[pl.ds(pl.multiple_of(place, TILE), TILE), :]
        for h in range(2):
            part = pl.ds(HALF * h, HALF)
            product = scale * contract_last(unit[side, part, :], other)
            odds = jnp.exp(product + shift)
            coeff = odds / (1.0 + odds)
            if weight is not None:
                count(weight, jnp.log1p(odds), coeff * product, coeff)
            total[side, part, :] += jnp.dot(coeff.astype(BF16), other, preferred_element_type=F32)

    first_core = jnp.where(core == 0, 1.0, 0.0).astype(F32)
    second_core = 1.0 - first_core
    to_pair.wait_recv()

    @pl.loop(0, ROWS // TILE)
    def _(q):
        work(1 - core, PARTNER + TILE * q, first_core)

    lane = lax.broadcasted_iota(jnp.int32, (8, 128), 1)
    row = lax.broadcasted_iota(jnp.int32, (8, 128), 0)

    def exchange(level, i):
        return pltpu.make_async_remote_copy(
            src_ref=share.at[level, 0],
            dst_ref=share.at[level, i],
            send_sem=share_send.at[level, i - 1],
            recv_sem=share_recv.at[level, i - 1],
            device_id=group(level, i),
            device_id_type=MESH,
        )

    def gathered(level):
        for i in (1, 2, 3):
            exchange(level, i).wait_recv()
        return (share[level, 0] + share[level, 2]) + (share[level, 1] + share[level, 3])

    def send_share(level, value):
        share[level, 0] = value
        for i in (1, 2, 3):
            exchange(level, i).start()

    def step(t, weight):
        link(t).wait_recv()
        hand_on(t).start()
        hand_on(t).wait_recv()
        work(t // PIECES, 2 * PIECE * t, weight)

    @pl.loop(0, STEPS - 1)
    def _(t):
        link(t).wait_send()

        @pl.when(t + WINDOW < STEPS)
        def _():
            link(t + WINDOW).start()

        @pl.when((t == PIECES) & (core == 1))
        def _():
            for q in range(4):
                to_skip(q).start()

        @pl.when(t == PIECES)
        def _():
            value = jnp.zeros((8, 128), F32)
            for i in range(3):
                value = jnp.where(lane == i, jnp.sum(sums[i]), value)
            send_share(0, value)

        for level in range(3):
            @pl.when(t == PIECES + 1 + level)
            def _():
                send_share(level + 1, gathered(level))

        step(t, jnp.where(t < PIECES, 1.0, 0.0).astype(F32))
        at = lax.rem(t, PIECES)

        @pl.when((t // PIECES == 1 - core) & (at >= 2) & (at < 6))
        def _():
            to_skip(at - 2).wait_recv()
            work(core, SKIP + TILE * (at - 2), second_core)

    def finish(side, j):
        rows = pl.ds(pl.multiple_of(PIECE * j, PIECE), PIECE)
        full = raw[side, rows, :].astype(F32)
        grad = total[side, rows, :]
        scaler = factor[side, rows, 0:1]
        inner = scaler * scaler * jnp.sum(full * grad, axis=-1, keepdims=True)
        result[side, rows, :] = (scale[:, 0:1] * scaler * (grad - full * inner)).astype(BF16)
        return pltpu.make_async_copy(
            result.at[side, rows], (image_grad, text_grad)[side].at[rows], out_sem.at[side, j]
        )

    @pl.loop(0, PIECES)
    def _(j):
        finish(0, j).start()

    answer = gathered(3)
    for i in range(3):
        picked = jnp.sum(jnp.where((lane == i) & (row == 0), answer, 0.0))
        totals[i] = picked / COUNT

    link(STEPS - 1).wait_send()
    step(STEPS - 1, None)

    @pl.loop(0, PIECES)
    def _(j):
        finish(1, j).start()

    to_pair.wait_send()
    for q in range(4):
        to_skip(q).wait_send()
    for level in range(4):
        for i in (1, 2, 3):
            exchange(level, i).wait_send()

    @pl.loop(0, STEPS)
    def _(t):
        hand_on(t).wait_send()

    @pl.loop(0, PIECES)
    def _(j):
        rows = pl.ds(pl.multiple_of(PIECE * j, PIECE), PIECE)
        for side in range(2):
            pltpu.make_async_copy(
                result.at[side, rows], (image_grad, text_grad)[side].at[rows], out_sem.at[side, j]
            ).wait()


def body(images, texts, positives, log_scale, bias):
    anywhere = pl.BlockSpec(memory_space=pl.ANY)
    smem = pl.BlockSpec(memory_space=pltpu.SMEM)
    dma = pltpu.SemaphoreType.DMA
    return pl.pallas_call(
        kernel,
        out_shape=(
            jax.ShapeDtypeStruct((ROWS, WIDTH), BF16),
            jax.ShapeDtypeStruct((ROWS, WIDTH), BF16),
            jax.ShapeDtypeStruct((3,), F32),
        ),
        in_specs=[anywhere, anywhere, pl.BlockSpec(memory_space=pltpu.VMEM), smem, smem],
        out_specs=(anywhere, anywhere, smem),
        scratch_shapes=[
            pltpu.VMEM((2, ROWS, WIDTH), BF16),
            pltpu.VMEM((2, ROWS, WIDTH), BF16),
            pltpu.VMEM((2, ROWS, 128), F32),
            pltpu.VMEM((2, ROWS, WIDTH), F32),
            pltpu.VMEM((SKIP + ROWS, WIDTH), BF16),
            pltpu.VMEM((2, ROWS, WIDTH), BF16),
            pltpu.VMEM((3, 8, 128), F32),
            pltpu.VMEM((4, 4, 8, 128), F32),
            dma((2,)),
            dma((STEPS,)),
            dma((STEPS,)),
            dma((STEPS,)),
            dma((STEPS,)),
            dma,
            dma,
            dma((4,)),
            dma((4,)),
            dma((4, 3)),
            dma((4, 3)),
            dma((2, PIECES)),
        ],
        compiler_params=pltpu.CompilerParams(
            collective_id=0, has_side_effects=True, vmem_limit_bytes=48 << 20
        ),
        cost_estimate=pl.CostEstimate(
            flops=15 * 2 * ROWS * ROWS * WIDTH, bytes_accessed=4 * ROWS * WIDTH * 2, transcendentals=0
        ),
    )(images, texts, positives, log_scale, bias)


def solution(mesh):
    return jax.shard_map(
        body,
        mesh=mesh,
        in_specs=(P(("blk", "dp"), None), P(("blk", "dp"), None), P(("blk", "dp"), None), P(), P()),
        out_specs=(P(("blk", "dp"), None), P(("blk", "dp"), None), P()),
        check_vma=False,
    )
```

time: 263 us -> 106 us (0.40)
  the two profiles are of different devices: /device:TPU:9 before, /device:TPU:1 now
where the time goes in v1:
time: 106 us; the launch traced here: 105 us
  Pallas kernels  97.7 us (92%)
  local copies, waits for them, and re-layouts  5.75 us (5%)
  between operations  1.94 us (2%)
    pallas_call x1, Pallas kernels, body(): pl.pallas_call(kernel, out_shape=(jax.ShapeDtypeStruct((ROWS, WIDTH), BF1...  97.7 us
    unnamed x9, local copies, waits for them, and re-layouts  5.75 us

profile of v1, /device:TPU:1, one launch (start us, length us, event | category | flops | bytes accessed | tf_op | source)
XLA Modules:
  0.0 105.4 jit_solution(12436181442880121873)
XLA Ops:
  1.9 0.0 copy-start
  1.9 1.3 %copy-done = bf16[512,1152]{1,0:T(8,128)(2,1)S(1)} copy-done((bf16[512,1152]{1,0:T(8,128)(2,1)S(1)}, bf16[512,1152]{1,0:T(8,128)(2,1)}, u32[]{:S(2)}) %copy-start) | copy-done | bytes 1179672
  3.2 0.0 copy-start.1
  3.2 1.3 %copy-done.1 = bf16[512,1152]{1,0:T(8,128)(2,1)S(1)} copy-done((bf16[512,1152]{1,0:T(8,128)(2,1)S(1)}, bf16[512,1152]{1,0:T(8,128)(2,1)}, u32[]{:S(2)}) %copy-start.1) | copy-done | bytes 1179672
  4.5 0.0 copy-start.2
  4.5 0.7 copy-done.2
  5.1 97.7 %shard_map.76 = (bf16[512,1152]{1,0:T(8,128)(2,1)S(1)}, bf16[512,1152]{1,0:T(8,128)(2,1)S(1)}, f32[3]{0:T(128)S(1)}) custom-call(bf16[512,1152]{1,0:T(8,128)(2,1)S(1)} %copy-done, bf16[512,1152]{1,0:T(8,128)(2,1)S(1)} %copy-done.1, s32[1,512]{1,0:T(1,128)S(1)} %copy-done.2, f32[1]{0:T(128)S(6)} %copy.11.log_scale, f32[1]{0:T(128)S(6)} %copy.12.bias), custom_call_target="tpu_custom_call" | custom-call | flops 9059696640 | bytes 4718592 | tf_op jit(solution)/shard_map/pallas_call | solution.py:324
  102.9 1.0 copy.13
  103.9 1.0 copy.14
  104.9 0.5 copy.15
Async XLA Ops:
  1.9 1.3 %copy-start = (bf16[512,1152]{1,0:T(8,128)(2,1)S(1)}, bf16[512,1152]{1,0:T(8,128)(2,1)}, u32[]{:S(2)}) copy-start(bf16[512,1152]{1,0:T(8,128)(2,1)} %images.1) | copy-start | bytes 3538948
  3.2 1.3 %copy-start.1 = (bf16[512,1152]{1,0:T(8,128)(2,1)S(1)}, bf16[512,1152]{1,0:T(8,128)(2,1)}, u32[]{:S(2)}) copy-start(bf16[512,1152]{1,0:T(8,128)(2,1)} %texts.1) | copy-start | bytes 3538948
  4.5 0.7 copy-start.2

commit v2 on v1

--- a/solution.py
+++ b/solution.py
@@ -13,16 +13,23 @@
 WIDTH = 1152
 COUNT = 131072.0
 N_BLK = 32
+N_DP = 8
 PIECE = 64
 PIECES = ROWS // PIECE
 STEPS = 2 * PIECES
 TILE = 128
 HALF = 256
-WINDOW = 3
 PARTNER = STEPS * 2 * PIECE
 SKIP = PARTNER + ROWS
 
 
+LEVELS = 4
+
+
+def others(level):
+    return range(1, 2) if level < 2 else range(1, 8)
+
+
 def contract_last(a, b):
     return lax.dot_general(a, b, (((1,), (1,)), ((), ())), preferred_element_type=F32)
 
@@ -37,7 +44,7 @@
 
 def kernel(
     images, texts, positives, log_scale, bias,
-    image_grad, text_grad, totals,
+    image_grad, text_grad, answer,
     raw, unit, factor, total, held, result, sums, share,
     load_sem, link_send, link_recv, pass_send, pass_recv, pair_send, pair_recv,
     skip_send, skip_recv, share_send, share_recv, out_sem,
@@ -45,6 +52,7 @@
     k = lax.axis_index("blk")
     p = lax.axis_index("dp")
     core = lax.rem(k, 2)
+    odd = lax.rem(k // 2, 2)
     pair = k + 1 - 2 * core
     skip = lax.rem(k - 3 + 6 * core + N_BLK, N_BLK)
 
@@ -56,21 +64,16 @@
 
     def group(level, i):
         if level == 0:
-            digit = lax.rem(k, 4)
-            return (k - digit + lax.rem(digit + i, 4), p)
+            return (pair, p)
         if level == 1:
-            digit = lax.rem(k // 4, 4)
-            return (k + 4 * (lax.rem(digit + i, 4) - digit), p)
+            return (k + 3 - 2 * lax.rem(k, 4), p)
         if level == 2:
-            digit = lax.rem(p, 4)
-            return (k, p - digit + lax.rem(digit + i, 4))
-        digit = 2 * (k // 16) + p // 4
-        other = lax.rem(digit + i, 4)
-        return (lax.rem(k, 16) + 16 * (other // 2), lax.rem(p, 4) + 4 * lax.rem(other, 2))
+            return (lax.rem(k + 4 * i, N_BLK), p)
+        return (k, lax.rem(p + i, N_DP))
 
     barrier = pltpu.get_barrier_semaphore()
     greeted = [(lax.rem(k + 2, N_BLK), p), (lax.rem(k - 2 + N_BLK, N_BLK), p), (pair, p), (skip, p)]
-    greeted += [group(level, i) for level in range(4) for i in (1, 2, 3)]
+    greeted += [group(level, i) for level in range(1, LEVELS) for i in others(level)]
     for device in greeted:
         pl.semaphore_signal(barrier, inc=1, device_id=device, device_id_type=MESH)
 
@@ -129,13 +132,11 @@
     normalize(1, 0)
     pl.semaphore_wait(barrier, len(greeted))
     link(0).start()
-    for j in range(1, WINDOW):
+
+    @pl.loop(1, PIECES)
+    def _(j):
         normalize(1, j)
         link(j).start()
-
-    @pl.loop(WINDOW, PIECES)
-    def _(j):
-        normalize(1, j)
 
     pl.when(core == 0)(to_pair.start)
     load(0).wait()
@@ -146,10 +147,17 @@
 
     pl.when(core == 1)(to_pair.start)
 
-    @pl.when(core == 0)
-    def _():
+    def send_skip():
         for q in range(4):
             to_skip(q).start()
+
+    pl.when(odd * core == 0)(send_skip)
+
+    @pl.when(odd == 1)
+    def _():
+        @pl.loop(PIECES, STEPS)
+        def _(t):
+            link(t).start()
 
     scale = jnp.exp(jnp.full((1, 128), log_scale[0], F32))
     shift = bias[0]
@@ -209,7 +217,6 @@
         work(1 - core, PARTNER + TILE * q, first_core)
 
     lane = lax.broadcasted_iota(jnp.int32, (8, 128), 1)
-    row = lax.broadcasted_iota(jnp.int32, (8, 128), 0)
 
     def exchange(level, i):
         return pltpu.make_async_remote_copy(
@@ -222,53 +229,75 @@
         )
 
     def gathered(level):
-        for i in (1, 2, 3):
+        for i in others(level):
             exchange(level, i).wait_recv()
-        return (share[level, 0] + share[level, 2]) + (share[level, 1] + share[level, 3])
+        parts = [share[level, i] for i in range(len(others(level)) + 1)]
+        while len(parts) > 1:
+            half = len(parts) // 2
+            parts = [parts[i] + parts[i + half] for i in range(half)]
+        return parts[0]
 
     def send_share(level, value):
         share[level, 0] = value
-        for i in (1, 2, 3):
+        for i in others(level):
             exchange(level, i).start()
 
-    def step(t, weight):
+    def arrive(t):
         link(t).wait_recv()
         hand_on(t).start()
+
+    def use(t, weight):
         hand_on(t).wait_recv()
         work(t // PIECES, 2 * PIECE * t, weight)
 
-    @pl.loop(0, STEPS - 1)
-    def _(t):
-        link(t).wait_send()
-
-        @pl.when(t + WINDOW < STEPS)
+    def order(s):
+        middle = lax.rem((s // 4 + 1) // 2, 2)
+        piece = (s + 4) // 2 + 4 * lax.rem(s + 1, 2)
+        return s + odd * middle * (piece - s)
+
+    @pl.loop(0, 13)
+    def _(s):
+        arrive(order(s))
+
+        @pl.when((odd == 0) & (s >= 2) & (s <= 8) & (lax.rem(s, 2) == 0))
         def _():
-            link(t + WINDOW).start()
-
-        @pl.when((t == PIECES) & (core == 1))
+            link(PIECES - 1 + s // 2).start()
+
+        @pl.when((odd == 0) & (s >= 10))
         def _():
-            for q in range(4):
-                to_skip(q).start()
-
-        @pl.when(t == PIECES)
+            link(PIECES - 6 + s).start()
+
+        pl.when((odd * core == 1) & (s == 7))(send_skip)
+
+        @pl.when(s > 0)
         def _():
-            value = jnp.zeros((8, 128), F32)
-            for i in range(3):
-                value = jnp.where(lane == i, jnp.sum(sums[i]), value)
-            send_share(0, value)
-
-        for level in range(3):
-            @pl.when(t == PIECES + 1 + level)
-            def _():
-                send_share(level + 1, gathered(level))
-
-        step(t, jnp.where(t < PIECES, 1.0, 0.0).astype(F32))
-        at = lax.rem(t, PIECES)
-
-        @pl.when((t // PIECES == 1 - core) & (at >= 2) & (at < 6))
+            t = order(s - 1)
+            use(t, 1.0 - (t // PIECES).astype(F32))
+
+        @pl.when(s >= 9)
         def _():
-            to_skip(at - 2).wait_recv()
-            work(core, SKIP + TILE * (at - 2), second_core)
+            to_skip(s - 9).wait_recv()
+            work(core, SKIP + TILE * (s - 9), second_core)
+
+    value = jnp.zeros((8, 128), F32)
+    for i in range(3):
+        value = jnp.where(lane == i, jnp.sum(sums[i]), value)
+    send_share(0, value)
+    use(12, None)
+    arrive(13)
+
+    @pl.when(odd == 0)
+    def _():
+        link(STEPS - 1).start()
+
+    send_share(1, gathered(0))
+    use(13, None)
+
+    def leave(side, j):
+        rows = pl.ds(pl.multiple_of(PIECE * j, PIECE), PIECE)
+        return pltpu.make_async_copy(
+            result.at[side, rows], (image_grad, text_grad)[side].at[rows], out_sem.at[side, j]
+        )
 
     def finish(side, j):
         rows = pl.ds(pl.multiple_of(PIECE * j, PIECE), PIECE)
@@ -277,59 +306,74 @@
         scaler = factor[side, rows, 0:1]
         inner = scaler * scaler * jnp.sum(full * grad, axis=-1, keepdims=True)
         result[side, rows, :] = (scale[:, 0:1] * scaler * (grad - full * inner)).astype(BF16)
-        return pltpu.make_async_copy(
-            result.at[side, rows], (image_grad, text_grad)[side].at[rows], out_sem.at[side, j]
-        )
+        leave(side, j).start()
+
+    arrive(14)
+    send_share(2, gathered(1))
 
     @pl.loop(0, PIECES)
     def _(j):
-        finish(0, j).start()
-
-    answer = gathered(3)
-    for i in range(3):
-        picked = jnp.sum(jnp.where((lane == i) & (row == 0), answer, 0.0))
-        totals[i] = picked / COUNT
-
-    link(STEPS - 1).wait_send()
-    step(STEPS - 1, None)
+        finish(0, j)
+
+    use(14, None)
+    arrive(15)
+    send_share(3, gathered(2))
+    use(15, None)
 
     @pl.loop(0, PIECES)
     def _(j):
-        finish(1, j).start()
-
+        finish(1, j)
+
+    found = gathered(3)
+    for i in range(3):
+        answer[i] = jnp.max(jnp.where(lane == i, found, -jnp.inf)) / COUNT
     to_pair.wait_send()
     for q in range(4):
         to_skip(q).wait_send()
-    for level in range(4):
-        for i in (1, 2, 3):
+    for level in range(LEVELS):
+        for i in others(level):
             exchange(level, i).wait_send()
 
     @pl.loop(0, STEPS)
     def _(t):
+        link(t).wait_send()
         hand_on(t).wait_send()
 
     @pl.loop(0, PIECES)
     def _(j):
-        rows = pl.ds(pl.multiple_of(PIECE * j, PIECE), PIECE)
-        for side in range(2):
-            pltpu.make_async_copy(
-                result.at[side, rows], (image_grad, text_grad)[side].at[rows], out_sem.at[side, j]
-            ).wait()
+        leave(0, j).wait()
+        leave(1, j).wait()
+
+
+def write(image, text, answer, image_grad, text_grad, totals, rows_held, totals_held, load_sem, store_sem):
+    loads = [pltpu.make_async_copy(answer, totals_held, load_sem.at[2, 0])]
+    stores = [pltpu.make_async_copy(totals_held, totals, store_sem.at[2, 0])]
+    for i, (source, target) in enumerate(((image, image_grad), (text, text_grad))):
+        for j in range(4):
+            rows = pl.ds(TILE * j, TILE)
+            loads.append(pltpu.make_async_copy(source.at[rows], rows_held.at[i, rows], load_sem.at[i, j]))
+            stores.append(pltpu.make_async_copy(rows_held.at[i, rows], target.at[rows], store_sem.at[i, j]))
+    for load in loads:
+        load.start()
+    for load, store in zip(loads, stores):
+        load.wait()
+        store.start()
+    for store in stores:
+        store.wait()
 
 
 def body(images, texts, positives, log_scale, bias):
-    anywhere = pl.BlockSpec(memory_space=pl.ANY)
+    hbm = pl.BlockSpec(memory_space=pltpu.HBM)
+    vmem = pl.BlockSpec(memory_space=pltpu.VMEM)
     smem = pl.BlockSpec(memory_space=pltpu.SMEM)
     dma = pltpu.SemaphoreType.DMA
-    return pl.pallas_call(
+    grad = jax.ShapeDtypeStruct((ROWS, WIDTH), BF16)
+    three = jax.ShapeDtypeStruct((3,), F32)
+    image, text, answer = pl.pallas_call(
         kernel,
-        out_shape=(
-            jax.ShapeDtypeStruct((ROWS, WIDTH), BF16),
-            jax.ShapeDtypeStruct((ROWS, WIDTH), BF16),
-            jax.ShapeDtypeStruct((3,), F32),
-        ),
-        in_specs=[anywhere, anywhere, pl.BlockSpec(memory_space=pltpu.VMEM), smem, smem],
-        out_specs=(anywhere, anywhere, smem),
+        out_shape=(grad, grad, three),
+        in_specs=[hbm, hbm, vmem, smem, smem],
+        out_specs=(hbm, hbm, smem),
         scratch_shapes=[
             pltpu.VMEM((2, ROWS, WIDTH), BF16),
             pltpu.VMEM((2, ROWS, WIDTH), BF16),
@@ -338,7 +382,7 @@
             pltpu.VMEM((SKIP + ROWS, WIDTH), BF16),
             pltpu.VMEM((2, ROWS, WIDTH), BF16),
             pltpu.VMEM((3, 8, 128), F32),
-            pltpu.VMEM((4, 4, 8, 128), F32),
+            pltpu.VMEM((LEVELS, 8, 8, 128), F32),
             dma((2,)),
             dma((STEPS,)),
             dma((STEPS,)),
@@ -348,17 +392,30 @@
             dma,
             dma((4,)),
             dma((4,)),
-            dma((4, 3)),
-            dma((4, 3)),
+            dma((LEVELS, 7)),
+            dma((LEVELS, 7)),
             dma((2, PIECES)),
         ],
         compiler_params=pltpu.CompilerParams(
-            collective_id=0, has_side_effects=True, vmem_limit_bytes=48 << 20
+            collective_id=0, has_side_effects=True, vmem_limit_bytes=58 << 20
         ),
         cost_estimate=pl.CostEstimate(
             flops=15 * 2 * ROWS * ROWS * WIDTH, bytes_accessed=4 * ROWS * WIDTH * 2, transcendentals=0
         ),
     )(images, texts, positives, log_scale, bias)
+    return pl.pallas_call(
+        write,
+        out_shape=(grad, grad, three),
+        in_specs=[hbm, hbm, hbm],
+        out_specs=(hbm, hbm, hbm),
+        scratch_shapes=[
+            pltpu.VMEM((2, ROWS, WIDTH), BF16),
+            pltpu.SMEM((3,), F32),
+            dma((3, 4)),
+            dma((3, 4)),
+        ],
+        compiler_params=pltpu.CompilerParams(vmem_limit_bytes=60 << 20),
+    )(image, text, answer)
 
 
 def solution(mesh):

time: 106 us -> 86.3 us (0.81)
  the two profiles are of different devices: /device:TPU:1 before, /device:TPU:9 now
where the time goes in v2:
time: 86.3 us; the launch traced here: 84.9 us
  Pallas kernels  82.9 us (96%)
  between operations  1.93 us (2%)
    pallas_call x1, Pallas kernels, body(): pl.pallas_call(kernel, out_shape=(grad, grad, three), in_specs=[hbm, hbm,...  80.4 us
    pallas_call x1, Pallas kernels, body(): pl.pallas_call(write, out_shape=(grad, grad, three), in_specs=[hbm, hbm,...  2.57 us

profile of v2, /device:TPU:9, one launch (start us, length us, event | category | flops | bytes accessed | tf_op | source)
XLA Modules:
  0.0 84.9 jit_solution(1542365149475393049)
XLA Ops:
  1.9 80.4 %shard_map.76 = (bf16[512,1152]{1,0:T(8,128)(2,1)}, bf16[512,1152]{1,0:T(8,128)(2,1)}, f32[3]{0:T(128)}) custom-call(bf16[512,1152]{1,0:T(8,128)(2,1)} %images.1, bf16[512,1152]{1,0:T(8,128)(2,1)} %texts.1, s32[1,512]{1,0:T(1,128)} %positives.1, f32[1]{0:T(128)S(6)} %copy.8.log_scale, f32[1]{0:T(128)S(6)} %copy.9.bias), custom_call_target="tpu_custom_call" | custom-call | flops 9059696640 | bytes 4718592 | tf_op jit(solution)/shard_map/pallas_call | solution.py:372
  82.3 2.6 %shard_map.77 = (bf16[512,1152]{1,0:T(8,128)(2,1)}, bf16[512,1152]{1,0:T(8,128)(2,1)}, f32[3]{0:T(128)}) custom-call(bf16[512,1152]{1,0:T(8,128)(2,1)} %get-tuple-element.6.image, bf16[512,1152]{1,0:T(8,128)(2,1)} %get-tuple-element.7.text, f32[3]{0:T(128)} %get-tuple-element.8.answer), custom_call_target="tpu_custom_call" | custom-call | tf_op jit(solution)/shard_map/pallas_call | solution.py:406

commit v3 on v2

--- a/solution.py
+++ b/solution.py
@@ -23,11 +23,12 @@
 SKIP = PARTNER + ROWS
 
 
-LEVELS = 4
+LEVELS = 6
+MIDDLE = (2, 3, 4)
 
 
 def others(level):
-    return range(1, 2) if level < 2 else range(1, 8)
+    return range(1, (2, 2, 2, 8, 4, 2)[level])
 
 
 def contract_last(a, b):
@@ -47,7 +48,7 @@
     image_grad, text_grad, answer,
     raw, unit, factor, total, held, result, sums, share,
     load_sem, link_send, link_recv, pass_send, pass_recv, pair_send, pair_recv,
-    skip_send, skip_recv, share_send, share_recv, out_sem,
+    skip_send, skip_recv, share_send, share_recv, out_sem, go_sem,
 ):
     k = lax.axis_index("blk")
     p = lax.axis_index("dp")
@@ -65,17 +66,26 @@
     def group(level, i):
         if level == 0:
             return (pair, p)
-        if level == 1:
-            return (k + 3 - 2 * lax.rem(k, 4), p)
+        if level == 1 or level == 5:
+            return (lax.rem(k + 6 - 12 * odd + N_BLK, N_BLK), p)
         if level == 2:
+            return (lax.rem(k + N_BLK // 2, N_BLK), p + 1 - 2 * lax.rem(p, 2))
+        if level == 3:
             return (lax.rem(k + 4 * i, N_BLK), p)
-        return (k, lax.rem(p + i, N_DP))
+        return (k, lax.rem(p + 2 * i, N_DP))
 
     barrier = pltpu.get_barrier_semaphore()
-    greeted = [(lax.rem(k + 2, N_BLK), p), (lax.rem(k - 2 + N_BLK, N_BLK), p), (pair, p), (skip, p)]
-    greeted += [group(level, i) for level in range(1, LEVELS) for i in others(level)]
+    greeted = [(lax.rem(k + 2, N_BLK), p), (lax.rem(k - 2 + N_BLK, N_BLK), p), (pair, p), (skip, p), group(1, 1)]
     for device in greeted:
         pl.semaphore_signal(barrier, inc=1, device_id=device, device_id_type=MESH)
+
+    @pl.when(odd == 1)
+    def _():
+        for level in MIDDLE:
+            for i in others(level):
+                pl.semaphore_signal(barrier, inc=1, device_id=group(level, i), device_id_type=MESH)
+
+    greetings = len(greeted) + odd * sum(len(others(level)) for level in MIDDLE)
 
     def link(t):
         second = t // PIECES
@@ -130,7 +140,7 @@
 
     load(1).wait()
     normalize(1, 0)
-    pl.semaphore_wait(barrier, len(greeted))
+    pl.semaphore_wait(barrier, greetings)
     link(0).start()
 
     @pl.loop(1, PIECES)
@@ -250,48 +260,60 @@
         hand_on(t).wait_recv()
         work(t // PIECES, 2 * PIECE * t, weight)
 
-    def order(s):
-        middle = lax.rem((s // 4 + 1) // 2, 2)
-        piece = (s + 4) // 2 + 4 * lax.rem(s + 1, 2)
-        return s + odd * middle * (piece - s)
-
-    @pl.loop(0, 13)
-    def _(s):
-        arrive(order(s))
-
-        @pl.when((odd == 0) & (s >= 2) & (s <= 8) & (lax.rem(s, 2) == 0))
-        def _():
-            link(PIECES - 1 + s // 2).start()
-
-        @pl.when((odd == 0) & (s >= 10))
-        def _():
-            link(PIECES - 6 + s).start()
-
-        pl.when((odd * core == 1) & (s == 7))(send_skip)
-
-        @pl.when(s > 0)
-        def _():
-            t = order(s - 1)
-            use(t, 1.0 - (t // PIECES).astype(F32))
-
-        @pl.when(s >= 9)
-        def _():
-            to_skip(s - 9).wait_recv()
-            work(core, SKIP + TILE * (s - 9), second_core)
-
-    value = jnp.zeros((8, 128), F32)
-    for i in range(3):
-        value = jnp.where(lane == i, jnp.sum(sums[i]), value)
-    send_share(0, value)
-    use(12, None)
-    arrive(13)
-
-    @pl.when(odd == 0)
-    def _():
-        link(STEPS - 1).start()
-
-    send_share(1, gathered(0))
-    use(13, None)
+    ahead = (lax.rem(k + 2, N_BLK), p)
+
+    @pl.loop(0, STEPS - 2)
+    def _(t):
+        arrive(t)
+
+        @pl.when((odd == 0) & (t == PIECES - 1))
+        def _():
+            pl.semaphore_wait(go_sem, 1)
+
+            @pl.loop(PIECES, STEPS)
+            def _(i):
+                link(i).start()
+
+        pl.when((odd * core == 1) & (t == PIECES - 1))(send_skip)
+
+        @pl.when(t > 0)
+        def _():
+            use(t - 1, jnp.where(t <= PIECES, 1.0, 0.0).astype(F32))
+
+        @pl.when((odd == 1) & (t == PIECES - 2))
+        def _():
+            pl.semaphore_signal(go_sem, inc=1, device_id=ahead, device_id_type=MESH)
+
+        q = t - 9 + 5 * core
+
+        @pl.when((q >= 0) & (q < 4))
+        def _():
+            to_skip(q).wait_recv()
+            work(core, SKIP + TILE * q, second_core)
+
+        @pl.when(t == PIECES)
+        def _():
+            value = jnp.zeros((8, 128), F32)
+            for i in range(3):
+                value = jnp.where(lane == i, jnp.sum(sums[i]), value)
+            send_share(0, value)
+
+        @pl.when((odd == 0) & (t == PIECES + 1))
+        def _():
+            send_share(1, gathered(0))
+
+        @pl.when((odd == 1) & (t == PIECES + 1))
+        def _():
+            share[1, 0] = gathered(0)
+
+        for level in MIDDLE:
+            @pl.when((odd == 1) & (t == PIECES + level))
+            def _():
+                send_share(level, gathered(level - 1))
+
+        @pl.when((odd == 1) & (t == PIECES + 5))
+        def _():
+            send_share(5, gathered(4))
 
     def leave(side, j):
         rows = pl.ds(pl.multiple_of(PIECE * j, PIECE), PIECE)
@@ -308,31 +330,41 @@
         result[side, rows, :] = (scale[:, 0:1] * scaler * (grad - full * inner)).astype(BF16)
         leave(side, j).start()
 
-    arrive(14)
-    send_share(2, gathered(1))
+    arrive(STEPS - 2)
+    use(STEPS - 3, None)
 
     @pl.loop(0, PIECES)
     def _(j):
         finish(0, j)
 
-    use(14, None)
-    arrive(15)
-    send_share(3, gathered(2))
-    use(15, None)
+    use(STEPS - 2, None)
+
+    @pl.when(odd == 0)
+    def _():
+        exchange(5, 1).wait_recv()
+        share[5, 0] = share[5, 1]
+
+    found = share[5, 0]
+    for i in range(3):
+        answer[i] = jnp.max(jnp.where(lane == i, found, -jnp.inf)) / COUNT
+    arrive(STEPS - 1)
+    use(STEPS - 1, None)
 
     @pl.loop(0, PIECES)
     def _(j):
         finish(1, j)
 
-    found = gathered(3)
-    for i in range(3):
-        answer[i] = jnp.max(jnp.where(lane == i, found, -jnp.inf)) / COUNT
     to_pair.wait_send()
     for q in range(4):
         to_skip(q).wait_send()
-    for level in range(LEVELS):
-        for i in others(level):
-            exchange(level, i).wait_send()
+    exchange(0, 1).wait_send()
+    pl.when(odd == 0)(exchange(1, 1).wait_send)
+
+    @pl.when(odd == 1)
+    def _():
+        for level in (*MIDDLE, 5):
+            for i in others(level):
+                exchange(level, i).wait_send()
 
     @pl.loop(0, STEPS)
     def _(t):
@@ -395,6 +427,7 @@
             dma((LEVELS, 7)),
             dma((LEVELS, 7)),
             dma((2, PIECES)),
+            pltpu.SemaphoreType.REGULAR,
         ],
         compiler_params=pltpu.CompilerParams(
             collective_id=0, has_side_effects=True, vmem_limit_bytes=58 << 20

time: 86.3 us -> 82.6 us (0.957)
  Pallas kernels: 82.9 us -> 79.7 us
    pallas_call x1, Pallas kernels: 80.4 us -> 77.1 us  [body(): pl.pallas_call(kernel, out_shape=(grad, grad, three), in_specs=[hbm, hbm,...]
where the time goes in v3:
time: 82.6 us; the launch traced here: 81.6 us
  Pallas kernels  79.7 us (96%)
  between operations  1.93 us (2%)
    pallas_call x1, Pallas kernels, body(): pl.pallas_call(kernel, out_shape=(grad, grad, three), in_specs=[hbm, hbm,...  77.1 us
    pallas_call x1, Pallas kernels, body(): pl.pallas_call(write, out_shape=(grad, grad, three), in_specs=[hbm, hbm,...  2.57 us

profile of v3, /device:TPU:9, one launch (start us, length us, event | category | flops | bytes accessed | tf_op | source)
XLA Modules:
  0.0 81.6 jit_solution(464584837605248500)
XLA Ops:
  1.9 77.1 %shard_map.76 = (bf16[512,1152]{1,0:T(8,128)(2,1)}, bf16[512,1152]{1,0:T(8,128)(2,1)}, f32[3]{0:T(128)}) custom-call(bf16[512,1152]{1,0:T(8,128)(2,1)} %images.1, bf16[512,1152]{1,0:T(8,128)(2,1)} %texts.1, s32[1,512]{1,0:T(1,128)} %positives.1, f32[1]{0:T(128)S(6)} %copy.8.log_scale, f32[1]{0:T(128)S(6)} %copy.9.bias), custom_call_target="tpu_custom_call" | custom-call | flops 9059696640 | bytes 4718592 | tf_op jit(solution)/shard_map/pallas_call | solution.py:404
  79.0 2.6 %shard_map.77 = (bf16[512,1152]{1,0:T(8,128)(2,1)}, bf16[512,1152]{1,0:T(8,128)(2,1)}, f32[3]{0:T(128)}) custom-call(bf16[512,1152]{1,0:T(8,128)(2,1)} %get-tuple-element.6.image, bf16[512,1152]{1,0:T(8,128)(2,1)} %get-tuple-element.7.text, f32[3]{0:T(128)} %get-tuple-element.8.answer), custom_call_target="tpu_custom_call" | custom-call | tf_op jit(solution)/shard_map/pallas_call | solution.py:439

commit v4 on v3

--- a/solution.py
+++ b/solution.py
@@ -23,12 +23,12 @@
 SKIP = PARTNER + ROWS
 
 
-LEVELS = 6
+LEVELS = 7
 MIDDLE = (2, 3, 4)
 
 
 def others(level):
-    return range(1, (2, 2, 2, 8, 4, 2)[level])
+    return range(1, (2, 2, 2, 8, 4, 2, 2)[level])
 
 
 def contract_last(a, b):
@@ -64,7 +64,7 @@
     load(0).start()
 
     def group(level, i):
-        if level == 0:
+        if level == 0 or level == 6:
             return (pair, p)
         if level == 1 or level == 5:
             return (lax.rem(k + 6 - 12 * odd + N_BLK, N_BLK), p)
@@ -75,17 +75,23 @@
         return (k, lax.rem(p + 2 * i, N_DP))
 
     barrier = pltpu.get_barrier_semaphore()
-    greeted = [(lax.rem(k + 2, N_BLK), p), (lax.rem(k - 2 + N_BLK, N_BLK), p), (pair, p), (skip, p), group(1, 1)]
+    greeted = [(lax.rem(k + 2, N_BLK), p), (lax.rem(k - 2 + N_BLK, N_BLK), p), (pair, p), (skip, p)]
     for device in greeted:
         pl.semaphore_signal(barrier, inc=1, device_id=device, device_id_type=MESH)
-
-    @pl.when(odd == 1)
+    lead = 1 - core
+    hub = lead * odd
+
+    @pl.when(lead == 1)
+    def _():
+        pl.semaphore_signal(barrier, inc=1, device_id=group(1, 1), device_id_type=MESH)
+
+    @pl.when(hub == 1)
     def _():
         for level in MIDDLE:
             for i in others(level):
                 pl.semaphore_signal(barrier, inc=1, device_id=group(level, i), device_id_type=MESH)
 
-    greetings = len(greeted) + odd * sum(len(others(level)) for level in MIDDLE)
+    greetings = len(greeted) + lead + hub * sum(len(others(level)) for level in MIDDLE)
 
     def link(t):
         second = t // PIECES
@@ -111,14 +117,20 @@
             device_id_type=MESH,
         )
 
-    to_pair = pltpu.make_async_remote_copy(
-        src_ref=unit.at[1 - core],
-        dst_ref=held.at[pl.ds(PARTNER, ROWS)],
-        send_sem=pair_send,
-        recv_sem=pair_recv,
-        device_id=(pair, p),
-        device_id_type=MESH,
-    )
+    def to_pair(q):
+        start = pl.multiple_of(TILE * q, TILE)
+        return pltpu.make_async_remote_copy(
+            src_ref=unit.at[1 - core, pl.ds(start, TILE)],
+            dst_ref=held.at[pl.ds(PARTNER + start, TILE)],
+            send_sem=pair_send.at[q],
+            recv_sem=pair_recv.at[q],
+            device_id=(pair, p),
+            device_id_type=MESH,
+        )
+
+    def send_pair():
+        for q in range(4):
+            to_pair(q).start()
 
     def to_skip(q):
         start = pl.multiple_of(TILE * q, TILE)
@@ -148,14 +160,14 @@
         normalize(1, j)
         link(j).start()
 
-    pl.when(core == 0)(to_pair.start)
+    pl.when(core == 0)(send_pair)
     load(0).wait()
 
     @pl.loop(0, PIECES)
     def _(j):
         normalize(0, j)
 
-    pl.when(core == 1)(to_pair.start)
+    pl.when(core == 1)(send_pair)
 
     def send_skip():
         for q in range(4):
@@ -218,14 +230,6 @@
                 count(weight, jnp.log1p(odds), coeff * product, coeff)
             total[side, part, :] += jnp.dot(coeff.astype(BF16), other, preferred_element_type=F32)
 
-    first_core = jnp.where(core == 0, 1.0, 0.0).astype(F32)
-    second_core = 1.0 - first_core
-    to_pair.wait_recv()
-
-    @pl.loop(0, ROWS // TILE)
-    def _(q):
-        work(1 - core, PARTNER + TILE * q, first_core)
-
     lane = lax.broadcasted_iota(jnp.int32, (8, 128), 1)
 
     def exchange(level, i):
@@ -276,6 +280,11 @@
 
         pl.when((odd * core == 1) & (t == PIECES - 1))(send_skip)
 
+        @pl.when((lead == 1) & (t == PIECES + 1))
+        def _():
+            share[1, 0] = gathered(0)
+            pl.when(odd == 0)(lambda: exchange(1, 1).start())
+
         @pl.when(t > 0)
         def _():
             use(t - 1, jnp.where(t <= PIECES, 1.0, 0.0).astype(F32))
@@ -284,36 +293,35 @@
         def _():
             pl.semaphore_signal(go_sem, inc=1, device_id=ahead, device_id_type=MESH)
 
-        q = t - 9 + 5 * core
+        second = t // PIECES
+        q = t - 4 - 5 * second
 
         @pl.when((q >= 0) & (q < 4))
         def _():
-            to_skip(q).wait_recv()
-            work(core, SKIP + TILE * q, second_core)
+            near = core == second
+            pl.when(near)(lambda: to_pair(q).wait_recv())
+            pl.when(jnp.logical_not(near))(lambda: to_skip(q).wait_recv())
+            place = PARTNER + ROWS * (core + second - 2 * core * second)
+            work(1 - second, place + TILE * q, 1.0 - second.astype(F32))
 
         @pl.when(t == PIECES)
         def _():
             value = jnp.zeros((8, 128), F32)
             for i in range(3):
                 value = jnp.where(lane == i, jnp.sum(sums[i]), value)
-            send_share(0, value)
-
-        @pl.when((odd == 0) & (t == PIECES + 1))
-        def _():
-            send_share(1, gathered(0))
-
-        @pl.when((odd == 1) & (t == PIECES + 1))
-        def _():
-            share[1, 0] = gathered(0)
+            share[0, 0] = value
+            pl.when(core == 1)(lambda: exchange(0, 1).start())
 
         for level in MIDDLE:
-            @pl.when((odd == 1) & (t == PIECES + level))
+            @pl.when((hub == 1) & (t == PIECES - 1 + level))
             def _():
                 send_share(level, gathered(level - 1))
 
-        @pl.when((odd == 1) & (t == PIECES + 5))
-        def _():
-            send_share(5, gathered(4))
+        @pl.when((hub == 1) & (t == PIECES + 4))
+        def _():
+            value = gathered(4)
+            send_share(5, value)
+            send_share(6, value)
 
     def leave(side, j):
         rows = pl.ds(pl.multiple_of(PIECE * j, PIECE), PIECE)
@@ -339,14 +347,11 @@
 
     use(STEPS - 2, None)
 
-    @pl.when(odd == 0)
+    @pl.when((lead == 1) & (odd == 0))
     def _():
         exchange(5, 1).wait_recv()
-        share[5, 0] = share[5, 1]
-
-    found = share[5, 0]
-    for i in range(3):
-        answer[i] = jnp.max(jnp.where(lane == i, found, -jnp.inf)) / COUNT
+        send_share(6, share[5, 1])
+
     arrive(STEPS - 1)
     use(STEPS - 1, None)
 
@@ -354,13 +359,22 @@
     def _(j):
         finish(1, j)
 
-    to_pair.wait_send()
+    @pl.when(core == 1)
+    def _():
+        exchange(6, 1).wait_recv()
+        share[6, 0] = share[6, 1]
+
+    found = share[6, 0]
+    for i in range(3):
+        answer[i] = jnp.max(jnp.where(lane == i, found, -jnp.inf)) / COUNT
     for q in range(4):
+        to_pair(q).wait_send()
         to_skip(q).wait_send()
-    exchange(0, 1).wait_send()
-    pl.when(odd == 0)(exchange(1, 1).wait_send)
-
-    @pl.when(odd == 1)
+    pl.when(core == 1)(lambda: exchange(0, 1).wait_send())
+    pl.when(lead == 1)(lambda: exchange(6, 1).wait_send())
+    pl.when(lead * (1 - odd) == 1)(lambda: exchange(1, 1).wait_send())
+
+    @pl.when(hub == 1)
     def _():
         for level in (*MIDDLE, 5):
             for i in others(level):
@@ -420,8 +434,8 @@
             dma((STEPS,)),
             dma((STEPS,)),
             dma((STEPS,)),
-            dma,
-            dma,
+            dma((4,)),
+            dma((4,)),
             dma((4,)),
             dma((4,)),
             dma((LEVELS, 7)),

time: 82.6 us -> 80.5 us (0.975); the launches traced: 81.6 us -> 80.4 us
  Pallas kernels: 79.7 us -> 78.4 us
    pallas_call x1, Pallas kernels: 77.1 us -> 75.9 us  [body(): pl.pallas_call(kernel, out_shape=(grad, grad, three), in_specs=[hbm, hbm,...]
where the time goes in v4:
time: 80.5 us; the launch traced here: 80.4 us
  Pallas kernels  78.4 us (97%)
  between operations  1.93 us (2%)
    pallas_call x1, Pallas kernels, body(): pl.pallas_call(kernel, out_shape=(grad, grad, three), in_specs=[hbm, hbm,...  75.9 us
    pallas_call x1, Pallas kernels, body(): pl.pallas_call(write, out_shape=(grad, grad, three), in_specs=[hbm, hbm,...  2.57 us

profile of v4, /device:TPU:9, one launch (start us, length us, event | category | flops | bytes accessed | tf_op | source)
XLA Modules:
  0.0 80.4 jit_solution(7317895420508344515)
XLA Ops:
  1.9 75.9 %shard_map.76 = (bf16[512,1152]{1,0:T(8,128)(2,1)}, bf16[512,1152]{1,0:T(8,128)(2,1)}, f32[3]{0:T(128)}) custom-call(bf16[512,1152]{1,0:T(8,128)(2,1)} %images.1, bf16[512,1152]{1,0:T(8,128)(2,1)} %texts.1, s32[1,512]{1,0:T(1,128)} %positives.1, f32[1]{0:T(128)S(6)} %copy.8.log_scale, f32[1]{0:T(128)S(6)} %copy.9.bias), custom_call_target="tpu_custom_call" | custom-call | flops 9059696640 | bytes 4718592 | tf_op jit(solution)/shard_map/pallas_call | solution.py:418
  77.8 2.6 %shard_map.77 = (bf16[512,1152]{1,0:T(8,128)(2,1)}, bf16[512,1152]{1,0:T(8,128)(2,1)}, f32[3]{0:T(128)}) custom-call(bf16[512,1152]{1,0:T(8,128)(2,1)} %get-tuple-element.6.image, bf16[512,1152]{1,0:T(8,128)(2,1)} %get-tuple-element.7.text, f32[3]{0:T(128)} %get-tuple-element.8.answer), custom_call_target="tpu_custom_call" | custom-call | tf_op jit(solution)/shard_map/pallas_call | solution.py:453

commit v5 on v4

--- a/solution.py
+++ b/solution.py
@@ -44,11 +44,11 @@
 
 
 def kernel(
-    images, texts, positives, log_scale, bias,
-    image_grad, text_grad, answer,
-    raw, unit, factor, total, held, result, sums, share,
+    images, texts, positives_in, log_scale_in, bias_in,
+    image_grad, text_grad, answer_out,
+    positives, log_scale, bias, answer, raw, unit, factor, total, held, result, sums, share,
     load_sem, link_send, link_recv, pass_send, pass_recv, pair_send, pair_recv,
-    skip_send, skip_recv, share_send, share_recv, out_sem, go_sem,
+    skip_send, skip_recv, share_send, share_recv, out_sem, answer_sem, go_sem,
 ):
     k = lax.axis_index("blk")
     p = lax.axis_index("dp")
@@ -60,8 +60,16 @@
     def load(side):
         return pltpu.make_async_copy((images, texts)[side], raw.at[side], load_sem.at[side])
 
+    small = [
+        pltpu.make_async_copy(source, target, load_sem.at[2 + i])
+        for i, (source, target) in enumerate(
+            ((positives_in, positives), (log_scale_in, log_scale), (bias_in, bias))
+        )
+    ]
     load(1).start()
     load(0).start()
+    for copy in small:
+        copy.start()
 
     def group(level, i):
         if level == 0 or level == 6:
@@ -181,6 +189,8 @@
         def _(t):
             link(t).start()
 
+    for copy in small:
+        copy.wait()
     scale = jnp.exp(jnp.full((1, 128), log_scale[0], F32))
     shift = bias[0]
     sums[...] = jnp.zeros_like(sums)
@@ -219,16 +229,19 @@
 
         total[0, cols, :] = contract_first(jnp.concatenate(halves, axis=0), unit[1])
 
+    def work_half(side, other, weight, h):
+        part = pl.ds(HALF * h, HALF)
+        product = scale * contract_last(unit[side, part, :], other)
+        odds = jnp.exp(product + shift)
+        coeff = odds / (1.0 + odds)
+        if weight is not None:
+            count(weight, jnp.log1p(odds), coeff * product, coeff)
+        total[side, part, :] += jnp.dot(coeff.astype(BF16), other, preferred_element_type=F32)
+
     def work(side, place, weight):
         other = held[pl.ds(pl.multiple_of(place, TILE), TILE), :]
         for h in range(2):
-            part = pl.ds(HALF * h, HALF)
-            product = scale * contract_last(unit[side, part, :], other)
-            odds = jnp.exp(product + shift)
-            coeff = odds / (1.0 + odds)
-            if weight is not None:
-                count(weight, jnp.log1p(odds), coeff * product, coeff)
-            total[side, part, :] += jnp.dot(coeff.astype(BF16), other, preferred_element_type=F32)
+            work_half(side, other, weight, h)
 
     lane = lax.broadcasted_iota(jnp.int32, (8, 128), 1)
 
@@ -353,11 +366,12 @@
         send_share(6, share[5, 1])
 
     arrive(STEPS - 1)
-    use(STEPS - 1, None)
-
-    @pl.loop(0, PIECES)
-    def _(j):
-        finish(1, j)
+    hand_on(STEPS - 1).wait_recv()
+    other = held[2 * PIECE * (STEPS - 1) : 2 * PIECE * STEPS, :]
+    for h in range(2):
+        work_half(1, other, None, h)
+        for j in range(PIECES // 2):
+            finish(1, PIECES // 2 * h + j)
 
     @pl.when(core == 1)
     def _():
@@ -367,6 +381,8 @@
     found = share[6, 0]
     for i in range(3):
         answer[i] = jnp.max(jnp.where(lane == i, found, -jnp.inf)) / COUNT
+    leave_answer = pltpu.make_async_copy(answer, answer_out, answer_sem)
+    leave_answer.start()
     for q in range(4):
         to_pair(q).wait_send()
         to_skip(q).wait_send()
@@ -389,6 +405,8 @@
     def _(j):
         leave(0, j).wait()
         leave(1, j).wait()
+
+    leave_answer.wait()
 
 
 def write(image, text, answer, image_grad, text_grad, totals, rows_held, totals_held, load_sem, store_sem):
@@ -410,17 +428,19 @@
 
 def body(images, texts, positives, log_scale, bias):
     hbm = pl.BlockSpec(memory_space=pltpu.HBM)
-    vmem = pl.BlockSpec(memory_space=pltpu.VMEM)
-    smem = pl.BlockSpec(memory_space=pltpu.SMEM)
     dma = pltpu.SemaphoreType.DMA
     grad = jax.ShapeDtypeStruct((ROWS, WIDTH), BF16)
     three = jax.ShapeDtypeStruct((3,), F32)
     image, text, answer = pl.pallas_call(
         kernel,
         out_shape=(grad, grad, three),
-        in_specs=[hbm, hbm, vmem, smem, smem],
-        out_specs=(hbm, hbm, smem),
+        in_specs=[hbm, hbm, hbm, hbm, hbm],
+        out_specs=(hbm, hbm, hbm),
         scratch_shapes=[
+            pltpu.VMEM((1, ROWS), jnp.int32),
+            pltpu.SMEM((1,), F32),
+            pltpu.SMEM((1,), F32),
+            pltpu.SMEM((3,), F32),
             pltpu.VMEM((2, ROWS, WIDTH), BF16),
             pltpu.VMEM((2, ROWS, WIDTH), BF16),
             pltpu.VMEM((2, ROWS, 128), F32),
@@ -429,7 +449,7 @@
             pltpu.VMEM((2, ROWS, WIDTH), BF16),
             pltpu.VMEM((3, 8, 128), F32),
             pltpu.VMEM((LEVELS, 8, 8, 128), F32),
-            dma((2,)),
+            dma((5,)),
             dma((STEPS,)),
             dma((STEPS,)),
             dma((STEPS,)),
@@ -441,6 +461,7 @@
             dma((LEVELS, 7)),
             dma((LEVELS, 7)),
             dma((2, PIECES)),
+            dma,
             pltpu.SemaphoreType.REGULAR,
         ],
         compiler_params=pltpu.CompilerParams(

time: 80.5 us -> 78.2 us (0.971)
  Pallas kernels: 78.4 us -> 76.1 us
    pallas_call x1, Pallas kernels: 75.9 us -> 73.6 us  [body(): pl.pallas_call(kernel, out_shape=(grad, grad, three), in_specs=[hbm, hbm,...]
where the time goes in v5:
time: 78.2 us; the launch traced here: 78.1 us
  Pallas kernels  76.1 us (97%)
  between operations  1.93 us (2%)
    pallas_call x1, Pallas kernels, body(): pl.pallas_call(kernel, out_shape=(grad, grad, three), in_specs=[hbm, hbm,...  73.6 us
    pallas_call x1, Pallas kernels, body(): pl.pallas_call(write, out_shape=(grad, grad, three), in_specs=[hbm, hbm,...  2.57 us

profile of v5, /device:TPU:9, one launch (start us, length us, event | category | flops | bytes accessed | tf_op | source)
XLA Modules:
  0.0 78.1 jit_solution(5562491212453934137)
XLA Ops:
  1.9 73.6 %shard_map.76 = (bf16[512,1152]{1,0:T(8,128)(2,1)}, bf16[512,1152]{1,0:T(8,128)(2,1)}, f32[3]{0:T(128)}) custom-call(bf16[512,1152]{1,0:T(8,128)(2,1)} %images.1, bf16[512,1152]{1,0:T(8,128)(2,1)} %texts.1, s32[1,512]{1,0:T(1,128)} %positives_in.1, f32[1]{0:T(128)S(6)} %copy.8.log_scale_in, f32[1]{0:T(128)S(6)} %copy.9.bias_in), custom_call_target="tpu_custom_call" | custom-call | flops 9059696640 | bytes 4718592 | tf_op jit(solution)/shard_map/pallas_call | solution.py:434
  75.5 2.6 %shard_map.77 = (bf16[512,1152]{1,0:T(8,128)(2,1)}, bf16[512,1152]{1,0:T(8,128)(2,1)}, f32[3]{0:T(128)}) custom-call(bf16[512,1152]{1,0:T(8,128)(2,1)} %get-tuple-element.6.image, bf16[512,1152]{1,0:T(8,128)(2,1)} %get-tuple-element.7.text, f32[3]{0:T(128)} %get-tuple-element.8.answer), custom_call_target="tpu_custom_call" | custom-call | tf_op jit(solution)/shard_map/pallas_call | solution.py:474

commit v6 on v5

--- a/solution.py
+++ b/solution.py
@@ -283,7 +283,7 @@
     def _(t):
         arrive(t)
 
-        @pl.when((odd == 0) & (t == PIECES - 1))
+        @pl.when((odd == 0) & (t == PIECES - 2))
         def _():
             pl.semaphore_wait(go_sem, 1)
 
@@ -360,12 +360,26 @@
 
     use(STEPS - 2, None)
 
+    for q in range(4):
+        to_pair(q).wait_send()
+        to_skip(q).wait_send()
+
+    @pl.loop(0, STEPS - 2)
+    def _(t):
+        link(t).wait_send()
+        hand_on(t).wait_send()
+
+    @pl.loop(0, PIECES)
+    def _(j):
+        leave(0, j).wait()
+
+    arrive(STEPS - 1)
+
     @pl.when((lead == 1) & (odd == 0))
     def _():
         exchange(5, 1).wait_recv()
         send_share(6, share[5, 1])
 
-    arrive(STEPS - 1)
     hand_on(STEPS - 1).wait_recv()
     other = held[2 * PIECE * (STEPS - 1) : 2 * PIECE * STEPS, :]
     for h in range(2):
@@ -383,9 +397,6 @@
         answer[i] = jnp.max(jnp.where(lane == i, found, -jnp.inf)) / COUNT
     leave_answer = pltpu.make_async_copy(answer, answer_out, answer_sem)
     leave_answer.start()
-    for q in range(4):
-        to_pair(q).wait_send()
-        to_skip(q).wait_send()
     pl.when(core == 1)(lambda: exchange(0, 1).wait_send())
     pl.when(lead == 1)(lambda: exchange(6, 1).wait_send())
     pl.when(lead * (1 - odd) == 1)(lambda: exchange(1, 1).wait_send())
@@ -396,14 +407,13 @@
             for i in others(level):
                 exchange(level, i).wait_send()
 
-    @pl.loop(0, STEPS)
+    @pl.loop(STEPS - 2, STEPS)
     def _(t):
         link(t).wait_send()
         hand_on(t).wait_send()
 
     @pl.loop(0, PIECES)
     def _(j):
-        leave(0, j).wait()
         leave(1, j).wait()
 
     leave_answer.wait()

time: 78.2 us -> 77.1 us (0.986)
  Pallas kernels: 76.1 us -> 75 us
    pallas_call x1, Pallas kernels: 73.6 us -> 72.4 us  [body(): pl.pallas_call(kernel, out_shape=(grad, grad, three), in_specs=[hbm, hbm,...]
where the time goes in v6:
time: 77.1 us; the launch traced here: 76.9 us
  Pallas kernels  75 us (97%)
  between operations  1.93 us (3%)
    pallas_call x1, Pallas kernels, body(): pl.pallas_call(kernel, out_shape=(grad, grad, three), in_specs=[hbm, hbm,...  72.4 us
    pallas_call x1, Pallas kernels, body(): pl.pallas_call(write, out_shape=(grad, grad, three), in_specs=[hbm, hbm,...  2.57 us

profile of v6, /device:TPU:9, one launch (start us, length us, event | category | flops | bytes accessed | tf_op | source)
XLA Modules:
  0.0 76.9 jit_solution(6747794732331813042)
XLA Ops:
  1.9 72.4 %shard_map.76 = (bf16[512,1152]{1,0:T(8,128)(2,1)}, bf16[512,1152]{1,0:T(8,128)(2,1)}, f32[3]{0:T(128)}) custom-call(bf16[512,1152]{1,0:T(8,128)(2,1)} %images.1, bf16[512,1152]{1,0:T(8,128)(2,1)} %texts.1, s32[1,512]{1,0:T(1,128)} %positives_in.1, f32[1]{0:T(128)S(6)} %copy.8.log_scale_in, f32[1]{0:T(128)S(6)} %copy.9.bias_in), custom_call_target="tpu_custom_call" | custom-call | flops 9059696640 | bytes 4718592 | tf_op jit(solution)/shard_map/pallas_call | solution.py:444
  74.4 2.6 %shard_map.77 = (bf16[512,1152]{1,0:T(8,128)(2,1)}, bf16[512,1152]{1,0:T(8,128)(2,1)}, f32[3]{0:T(128)}) custom-call(bf16[512,1152]{1,0:T(8,128)(2,1)} %get-tuple-element.6.image, bf16[512,1152]{1,0:T(8,128)(2,1)} %get-tuple-element.7.text, f32[3]{0:T(128)} %get-tuple-element.8.answer), custom_call_target="tpu_custom_call" | custom-call | tf_op jit(solution)/shard_map/pallas_call | solution.py:484

commit v7 on v6

--- a/solution.py
+++ b/solution.py
@@ -66,7 +66,11 @@
             ((positives_in, positives), (log_scale_in, log_scale), (bias_in, bias))
         )
     ]
-    load(1).start()
+    first, rest = pl.ds(0, PIECE), pl.ds(PIECE, ROWS - PIECE)
+    load_first = pltpu.make_async_copy(texts.at[first], raw.at[1, first], load_sem.at[5])
+    load_rest = pltpu.make_async_copy(texts.at[rest], raw.at[1, rest], load_sem.at[1])
+    load_first.start()
+    load_rest.start()
     load(0).start()
     for copy in small:
         copy.start()
@@ -158,10 +162,11 @@
         unit[side, rows, :] = (full * scaler).astype(BF16)
         factor[side, rows, :] = jnp.broadcast_to(scaler, (PIECE, 128))
 
-    load(1).wait()
+    load_first.wait()
     normalize(1, 0)
     pl.semaphore_wait(barrier, greetings)
     link(0).start()
+    load_rest.wait()
 
     @pl.loop(1, PIECES)
     def _(j):
@@ -459,7 +464,7 @@
             pltpu.VMEM((2, ROWS, WIDTH), BF16),
             pltpu.VMEM((3, 8, 128), F32),
             pltpu.VMEM((LEVELS, 8, 8, 128), F32),
-            dma((5,)),
+            dma((6,)),
             dma((STEPS,)),
             dma((STEPS,)),
             dma((STEPS,)),

time: 77.1 us -> 77.1 us (level)
  no operation moved by 1% of the time
where the time goes in v7:
time: 77.1 us; the launch traced here: 76.9 us
  Pallas kernels  75 us (97%)
  between operations  1.93 us (3%)
    pallas_call x1, Pallas kernels, body(): pl.pallas_call(kernel, out_shape=(grad, grad, three), in_specs=[hbm, hbm,...  72.5 us
    pallas_call x1, Pallas kernels, body(): pl.pallas_call(write, out_shape=(grad, grad, three), in_specs=[hbm, hbm,...  2.57 us

profile of v7, /device:TPU:9, one launch (start us, length us, event | category | flops | bytes accessed | tf_op | source)
XLA Modules:
  0.0 76.9 jit_solution(11573689772107329373)
XLA Ops:
  1.9 72.5 %shard_map.76 = (bf16[512,1152]{1,0:T(8,128)(2,1)}, bf16[512,1152]{1,0:T(8,128)(2,1)}, f32[3]{0:T(128)}) custom-call(bf16[512,1152]{1,0:T(8,128)(2,1)} %images.1, bf16[512,1152]{1,0:T(8,128)(2,1)} %texts.1, s32[1,512]{1,0:T(1,128)} %positives_in.1, f32[1]{0:T(128)S(6)} %copy.8.log_scale_in, f32[1]{0:T(128)S(6)} %copy.9.bias_in), custom_call_target="tpu_custom_call" | custom-call | flops 9059696640 | bytes 4718592 | tf_op jit(solution)/shard_map/pallas_call | solution.py:449
  74.4 2.6 %shard_map.77 = (bf16[512,1152]{1,0:T(8,128)(2,1)}, bf16[512,1152]{1,0:T(8,128)(2,1)}, f32[3]{0:T(128)}) custom-call(bf16[512,1152]{1,0:T(8,128)(2,1)} %get-tuple-element.6.image, bf16[512,1152]{1,0:T(8,128)(2,1)} %get-tuple-element.7.text, f32[3]{0:T(128)} %get-tuple-element.8.answer), custom_call_target="tpu_custom_call" | custom-call | tf_op jit(solution)/shard_map/pallas_call | solution.py:489
